TPU v7x, 256 devices: a whole 4x4x8 slice. The times are simulated.
256 devices in a mesh: seg: 8 (over z), blk: 32 (over x, y, core).
Axes of the slice: x: 4, y: 4, z: 8, core: 2. Of those that a mesh axis runs over, the one named last changes fastest.
Arguments:
- train_acts: bfloat16 [8, 4096, 512], P('seg', 'blk'), may hold values from -6 to 6
- train_grads: bfloat16 [8, 4096, 16384], P('seg', 'blk'), may hold values from -0.0059814453 to 0.0059814453
- counts: int32 [32], replicated, may hold values from 1 to 2, as said below
- basis_in: bfloat16 [8, 1, 512, 512], P('seg'), may hold values from -1 to 1, as said below
- basis_out: bfloat16 [8, 32, 512, 512], P('seg', 'blk'), may hold values from -1 to 1, as said below
- eigenvalues: bfloat16 [8, 32, 512, 512], P('seg', 'blk'), may hold values from 0.049804688 to 5
- back_weight: bfloat16 [8, 32, 512, 512], P('seg', 'blk'), may hold values from -0.25 to 0.25
- derivative: bfloat16 [8, 4, 32, 16384], P('seg', None, None, 'blk'), may hold values from 0 to 1
- query_acts: bfloat16 [8, 4, 32, 512], P('seg'), may hold values from -6 to 6
- query_top: bfloat16 [4, 32, 16384], P(None, None, 'blk'), may hold values from -0.0059814453 to 0.0059814453
Outputs:
- scores: float32 [4, 64], P(None, 'blk')
Inputs may be any that keep to these rules, and one draw needn't show every extreme that they name: In each pair of indices 2k and 2k+1 of blk one count is 2 and the other 1, so all counts add up to 48; slots below a device's count are valid. `basis_in`: each 512 x 512 matrix is orthogonal up to rounding. `basis_out`: each 512 x 512 matrix is orthogonal up to rounding.
All inputs are finite; a program needn't handle non-finite values.
Results may differ from a plain program's by a relative error of at most 0.015.
Values may be sent and summed in bfloat16 or wider, within the bound.
No kernel may reach another device: no remote copies, remote signals or barrier semaphores. Data moves between devices by JAX's collectives and lax.ppermute only.
A program may use at most 64 MiB of HBM per device.

v0:
```python
import math

import jax
import jax.numpy as jnp
from jax import lax
from jax.sharding import PartitionSpec as P

TB = 64
SLOTS = 2


damping = 0.05


def passed_along(value, axis, steps):
    count = lax.axis_size(axis)
    first, last = (max(0, -steps), min(count, count - steps))
    return lax.ppermute(value, axis, [(source, source + steps) for source in range(first, last)])


def advance(current, weight, derivs):
    queries, query_tok, blk_width = current.shape
    mixed = jnp.dot(
        current.reshape(queries * query_tok, blk_width), weight, preferred_element_type=jnp.float32
    )
    mixed = mixed.reshape(queries, query_tok, blk_width)
    return (current.astype(jnp.float32) + mixed * derivs.astype(jnp.float32)).astype(jnp.bfloat16)


def precondition(current, acts_seg, inner_basis, outer_basis, eigen_block):
    queries, query_tok, blk_width = current.shape
    in_slices = inner_basis.shape[0]
    in_width = in_slices * blk_width
    rot_err = jnp.dot(
        current.reshape(queries * query_tok, blk_width),
        outer_basis,
        preferred_element_type=jnp.float32,
    )
    rot_err = rot_err.astype(jnp.bfloat16).reshape(queries, query_tok, blk_width)
    act_split = acts_seg.reshape(queries, query_tok, in_slices, blk_width)
    rot_acts = jnp.einsum(
        "qtid,ide->qtie", act_split, inner_basis, preferred_element_type=jnp.float32
    ).astype(jnp.bfloat16)
    core_raw = jnp.einsum("qtd,qtie->qdie", rot_err, rot_acts, preferred_element_type=jnp.float32)
    core_raw = core_raw.reshape(queries, blk_width, in_width)
    scaled_core = (core_raw / (eigen_block.astype(jnp.float32)[None] + damping)).astype(
        jnp.bfloat16
    )
    left_prod = jnp.einsum(
        "cd,qdf->qcf", outer_basis, scaled_core, preferred_element_type=jnp.float32
    ).astype(jnp.bfloat16)
    left_split = left_prod.reshape(queries, blk_width, in_slices, blk_width)
    precond = jnp.einsum(
        "qcie,ife->qcif", left_split, inner_basis, preferred_element_type=jnp.float32
    )
    return precond.astype(jnp.bfloat16).reshape(queries, blk_width, in_width)


def block_scores(grad_rows, act_rows, precond, slot_tokens):
    row_count = grad_rows.shape[0]
    group_count = max(row_count // slot_tokens, 1)
    group_rows = row_count // group_count
    batch_groups = math.gcd(group_count, 8)
    grad_groups = grad_rows.reshape(
        group_count // batch_groups, batch_groups, group_rows, grad_rows.shape[1]
    )
    act_groups = act_rows.reshape(
        group_count // batch_groups, batch_groups, group_rows, act_rows.shape[1]
    )

    def one_batch(operands):
        grad_block, act_block = operands
        outer_prod = jnp.einsum(
            "btd,bte->bde", grad_block, act_block, preferred_element_type=jnp.float32
        ).astype(jnp.bfloat16)
        return jnp.einsum("bde,qde->bq", outer_prod, precond, preferred_element_type=jnp.float32)

    partial_scores = lax.map(one_batch, (grad_groups, act_groups))
    return (partial_scores.reshape(group_count, precond.shape[0]), group_rows)


def body(
    train_acts,
    train_grads,
    counts,
    basis_in,
    basis_out,
    eigenvalues,
    back_weight,
    derivative,
    query_acts,
    query_top,
):
    seg_count = lax.axis_size("seg")
    seg_index = lax.axis_index("seg")
    blk_index = lax.axis_index("blk")
    n_slot = lax.axis_size("blk") * SLOTS
    slot_ids = jnp.arange(n_slot, dtype=jnp.int32)
    current = query_top
    for relay_step in range(seg_count - 1):
        moved = advance(current, back_weight[0, 0], derivative[0])
        arrived = passed_along(moved, "seg", -1)
        current = jnp.where(seg_index == seg_count - 2 - relay_step, arrived, current)
    precond = precondition(current, query_acts[0], basis_in[0], basis_out[0, 0], eigenvalues[0, 0])
    exchanged = lax.all_to_all(train_grads, "blk", split_axis=2, concat_axis=1, tiled=True)
    grad_rows = exchanged[0]
    scores_part, group_rows = block_scores(
        grad_rows, lax.all_gather(train_acts, "blk", axis=1, tiled=True)[0], precond, TB
    )
    slot_of = jnp.arange(scores_part.shape[0], dtype=jnp.int32) * group_rows // TB
    placement = (slot_of[:, None] == slot_ids[None, :]).astype(jnp.float32)
    local_scores = jnp.dot(scores_part.T, placement, precision=lax.Precision.HIGHEST)
    mine = lax.psum_scatter(local_scores, "blk", scatter_dimension=1, tiled=True)
    mine = lax.psum(mine, "seg")
    own_valid = (jnp.arange(SLOTS, dtype=jnp.int32) < counts[blk_index]).astype(jnp.float32)
    return mine * own_valid[None, :]


def solution(mesh):
    in_specs = (
        P("seg", "blk", None),
        P("seg", "blk", None),
        P(),
        P("seg", None, None, None),
        P("seg", "blk", None, None),
        P("seg", "blk", None, None),
        P("seg", "blk", None, None),
        P("seg", None, None, "blk"),
        P("seg", None, None, None),
        P(None, None, "blk"),
    )
    out_specs = P(None, "blk")
    return jax.shard_map(body, mesh=mesh, in_specs=in_specs, out_specs=out_specs, check_vma=False)
```

profile of v0, /device:TPU:1, one launch (start us, length us, event | category | flops | bytes accessed | tf_op | source)
XLA Modules:
  0.0 424.6 jit_solution(13704850619412253560)
XLA Ops:
  10.0 5.4 %collective-permute-done = bf16[4,32,512]{2,1,0:T(8,128)(2,1)S(1)} collective-permute-done((bf16[4,32,512]{2,1,0:T(8,128)(2,1)S(1)}, bf16[4,32,512]{2,1,0:T(8,128)(2,1)S(1)}, u32[]{:S(2)}, u32[]{:S(2)}) %collective-permute-start) | collective-permute-done | bytes 131104 | tf_op jit(solution)/shard_map/ppermute | solution.py:18
  18.9 17.8 %copy.30 = bf16[1,128,16384]{1,0,2:T(2,128)(2,1)} copy(bf16[1,128,16384]{2,1,0:T(8,128)(2,1)} %param.13) | data formatting | bytes 8388608 | tf_op args[1]
  37.2 90.6 %reduce = bf16[16384,128]{1,0:T(8,128)(2,1)} reduce(bf16[16384,1,128]{2,1,0:T(2,128)(2,1)} %bitcast.120, bf16[]{:T(256)} %broadcast.54), dimensions={1}, to_apply=%bitcast.101.reduce_sub_computation | reduce | bytes 8388610
  127.8 6.9 %reshape.111 = bf16[32,2,32768]{2,1,0:T(2,128)(2,1)} reshape(bf16[16384,128]{1,0:T(8,128)(2,1)} %reduce) | data formatting | bytes 8388608
  134.7 9.3 %all-to-all-start = ((bf16[32,2,32768]{2,1,0:T(2,128)(2,1)}), bf16[32,2,32768]{2,1,0:T(2,128)(2,1)}, u32[]{:S(2)}, u32[]{:S(2)}) async-start(bf16[32,2,32768]{2,1,0:T(2,128)(2,1)} %reshape.111), calls=%async_computation | async-start | bytes 8388608 | tf_op jit(solution)/shard_map/all_to_all | solution.py:105
  145.7 6.7 %collective-permute-done.2 = bf16[4,32,512]{2,1,0:T(8,128)(2,1)S(1)} collective-permute-done((bf16[4,32,512]{2,1,0:T(8,128)(2,1)S(1)}, bf16[4,32,512]{2,1,0:T(8,128)(2,1)S(1)}, u32[]{:S(2)}, u32[]{:S(2)}) %collective-permute-start.2) | collective-permute-done | bytes 131104 | tf_op jit(solution)/shard_map/ppermute | solution.py:18
  154.0 5.2 %collective-permute-done.3 = bf16[4,32,512]{2,1,0:T(8,128)(2,1)S(1)} collective-permute-done((bf16[4,32,512]{2,1,0:T(8,128)(2,1)S(1)}, bf16[4,32,512]{2,1,0:T(8,128)(2,1)S(1)}, u32[]{:S(2)}, u32[]{:S(2)}) %collective-permute-start.3) | collective-permute-done | bytes 131104 | tf_op jit(solution)/shard_map/ppermute | solution.py:18
  160.7 6.4 %collective-permute-done.4 = bf16[4,32,512]{2,1,0:T(8,128)(2,1)S(1)} collective-permute-done((bf16[4,32,512]{2,1,0:T(8,128)(2,1)S(1)}, bf16[4,32,512]{2,1,0:T(8,128)(2,1)S(1)}, u32[]{:S(2)}, u32[]{:S(2)}) %collective-permute-start.4) | collective-permute-done | bytes 131104 | tf_op jit(solution)/shard_map/ppermute | solution.py:18
  168.9 6.2 %collective-permute-done.5 = bf16[4,32,512]{2,1,0:T(8,128)(2,1)S(1)} collective-permute-done((bf16[4,32,512]{2,1,0:T(8,128)(2,1)S(1)}, bf16[4,32,512]{2,1,0:T(8,128)(2,1)S(1)}, u32[]{:S(2)}, u32[]{:S(2)}) %collective-permute-start.5) | collective-permute-done | bytes 131104 | tf_op jit(solution)/shard_map/ppermute | solution.py:18
  182.6 3.2 fusion.13
  185.8 2.9 fusion.10
  190.3 6.0 %all-to-all-done = bf16[32,2,32768]{2,1,0:T(2,128)(2,1)} async-done(((bf16[32,2,32768]{2,1,0:T(2,128)(2,1)}), bf16[32,2,32768]{2,1,0:T(2,128)(2,1)}, u32[]{:S(2)}, u32[]{:S(2)}) %all-to-all-start) | async-done | bytes 4194336 | tf_op jit(solution)/shard_map/all_to_all | solution.py:105
  196.3 19.8 %reshape.112 = bf16[16384,1,128]{2,1,0:T(2,128)(2,1)} reshape(bf16[32,2,32768]{2,1,0:T(2,128)(2,1)} %all-to-all-done) | data formatting | bytes 8388608
  216.1 5.8 %copy.40 = bf16[1,128,16384]{1,2,0:T(8,128)(2,1)} copy(bf16[1,128,16384]{1,0,2:T(2,128)(2,1)} %bitcast.121) | data formatting | bytes 8388608
  221.9 6.5 %copy.31 = bf16[1,32,128,512]{3,2,1,0:T(8,128)(2,1)} copy(bf16[1,32,128,512]{2,3,1,0:T(8,128)(2,1)} %bitcast.122) | data formatting | bytes 8388608 | tf_op jit(solution)/shard_map/all_to_all | solution.py:105
  228.4 50.9 %while.10 = (s32[]{:T(128)}, f32[8,8,4]{1,0,2:T(8,128)S(1)}, bf16[8,8,64,512]{3,2,1,0:T(8,128)(2,1)}, bf16[8,8,64,512]{3,2,1,0:T(8,128)(2,1)}, bf16[4,512,512]{2,0,1:T(4,128)(2,1)S(1)}, /*index=5*/s32[]{:T(128)}, s32[]{:T(128)}) while((s32[]{:T(128)}, f32[8,8,4]{1,0,2:T(8,128)S(1)}, bf16[8,8,64,512]{3,2,1,0:T(8,128)(2,1)}, ...), condition=%wide.region_1.2_spmd, body=%wide.region_0.1_spmd.sunk | while | flops 287309824 | bytes 11535825 | solution.py:78
  230.9 3.8 fusion.61
  234.8 2.5 convolution_convert_fusion.4
  237.3 3.8 fusion.61
  241.1 2.5 convolution_convert_fusion.4
  243.6 3.8 fusion.61
  247.5 2.5 convolution_convert_fusion.4
  250.0 3.8 fusion.61
  253.9 2.5 convolution_convert_fusion.4
  256.4 3.8 fusion.61
  260.2 2.5 convolution_convert_fusion.4
  262.7 3.8 fusion.61
  269.1 3.8 fusion.61
  272.9 2.5 convolution_convert_fusion.4
  275.4 3.8 fusion.61
  279.7 120.0 %all-reduce = f32[4,64]{0,1:T(8,128)S(1)} all-reduce(f32[4,64]{0,1:T(8,128)S(1)} %fusion.41), channel_id=2, replica_groups=mesh['seg'=8,'blk'=32] {'blk'}, use_global_device_ids=true, to_apply=%region_2.3.clone | all-reduce | flops 256 | bytes 2048
  400.4 16.8 %psum.7 = f32[4,2]{0,1:T(2,128)S(1)} all-reduce(f32[4,2]{0,1:T(2,128)S(1)} %constant_dynamic-slice_fusion), channel_id=1, replica_groups=mesh['seg'=8,'blk'=32] {'seg'}, use_global_device_ids=true, to_apply=%region_3.4 | all-reduce | flops 8 | bytes 64 | tf_op jit(solution)/shard_map/psum | solution.py:114
  (63 shorter events, 29.0 us)
Async XLA Ops:
  6.5 175.8 %copy-start = (bf16[1,1,512,512]{3,2,1,0:T(8,128)(2,1)S(1)}, bf16[1,1,512,512]{3,2,1,0:T(8,128)(2,1)}, u32[]{:S(2)}) copy-start(bf16[1,1,512,512]{3,2,1,0:T(8,128)(2,1)} %param.16) | copy-start | bytes 1572868
  6.5 221.9 %all-gather.2.cloned.1.call-start = ((), (), s32[]{:S(2)}) async-start(), calls=%async_computation.1 | async-start | bytes 4325376 | tf_op jit(solution)/shard_map/all_gather | solution.py:108
  8.6 6.7 %collective-permute-start = (bf16[4,32,512]{2,1,0:T(8,128)(2,1)S(1)}, bf16[4,32,512]{2,1,0:T(8,128)(2,1)S(1)}, u32[]{:S(2)}, u32[]{:S(2)}) collective-permute-start(bf16[4,32,512]{2,1,0:T(8,128)(2,1)S(1)} %fusion.15), channel_id=1, source_target_pairs={{32,0},{64,32},{96,64},{128,96},{160,128},{192,160},{224,192},{33,... | collective-permute-start | bytes 393224 | tf_op jit(solution)/shard_map/ppermute | solution.py:18
  17.6 126.5 %collective-permute-start.1 = (bf16[4,32,512]{2,1,0:T(8,128)(2,1)S(1)}, bf16[4,32,512]{2,1,0:T(8,128)(2,1)S(1)}, u32[]{:S(2)}, u32[]{:S(2)}) collective-permute-start(bf16[4,32,512]{2,1,0:T(8,128)(2,1)S(1)} %add_convert_fusion.5), channel_id=1, source_target_pairs={{32,0},{64,32},{96,64},{128,96},{160,128},{192,160},{224,192},{33,... | collective-permute-start | bytes 393224 | tf_op jit(solution)/shard_map/ppermute | solution.py:18
  134.7 9.4 %copy-start.1 = (bf16[1,1,512,512]{3,2,1,0:T(8,128)(2,1)S(1)}, bf16[1,1,512,512]{3,2,1,0:T(8,128)(2,1)}, u32[]{:S(2)}) copy-start(bf16[1,1,512,512]{3,2,1,0:T(8,128)(2,1)} %param.18) | copy-start | bytes 1572868
  134.7 9.4 %copy-start.2 = (bf16[1,4,32,512]{3,2,1,0:T(8,128)(2,1)S(1)}, bf16[1,4,32,512]{3,2,1,0:T(8,128)(2,1)}, u32[]{:S(2)}) copy-start(bf16[1,4,32,512]{3,2,1,0:T(8,128)(2,1)} %param.19) | copy-start | bytes 393220
  134.7 61.6 %all-to-all-start = ((bf16[32,2,32768]{2,1,0:T(2,128)(2,1)}), bf16[32,2,32768]{2,1,0:T(2,128)(2,1)}, u32[]{:S(2)}, u32[]{:S(2)}) async-start(bf16[32,2,32768]{2,1,0:T(2,128)(2,1)} %reshape.111), calls=%async_computation | async-start | bytes 8388608 | tf_op jit(solution)/shard_map/all_to_all | solution.py:105
  144.1 24.7 %copy-start.3 = (bf16[1,1,512,512]{3,2,1,0:T(8,128)(2,1)S(1)}, bf16[1,1,512,512]{3,2,1,0:T(8,128)(2,1)}, u32[]{:S(2)}) copy-start(bf16[1,1,512,512]{3,2,1,0:T(8,128)(2,1)} %param.17) | copy-start | bytes 1572868
  144.1 32.7 %copy-start.5 = (bf16[1,4,32,512]{3,2,1,0:T(8,128)(2,1)S(1)}, bf16[1,4,32,512]{3,2,1,0:T(8,128)(2,1)}, u32[]{:S(2)}) copy-start(bf16[1,4,32,512]{3,2,1,0:T(8,128)(2,1)} %param.20) | copy-start | bytes 393220
  144.1 34.0 %copy-start.7 = (u32[256]{0:T(256)S(1)}, u32[256]{0:T(256)}, u32[]{:S(2)}) copy-start(u32[256]{0:T(256)} %constant.64) | copy-start | bytes 3076
  144.1 35.3 %copy-start.6 = (s32[32]{0:T(128)S(1)}, s32[32]{0:T(128)}, u32[]{:S(2)}) copy-start(s32[32]{0:T(128)} %param.14) | copy-start | bytes 388
  144.4 8.0 %collective-permute-start.2 = (bf16[4,32,512]{2,1,0:T(8,128)(2,1)S(1)}, bf16[4,32,512]{2,1,0:T(8,128)(2,1)S(1)}, u32[]{:S(2)}, u32[]{:S(2)}) collective-permute-start(bf16[4,32,512]{2,1,0:T(8,128)(2,1)S(1)} %add_convert_fusion.4), channel_id=1, source_target_pairs={{32,0},{64,32},{96,64},{128,96},{160,128},{192,160},{224,192},{33,... | collective-permute-start | bytes 393224 | tf_op jit(solution)/shard_map/ppermute | solution.py:18
  152.7 6.5 %collective-permute-start.3 = (bf16[4,32,512]{2,1,0:T(8,128)(2,1)S(1)}, bf16[4,32,512]{2,1,0:T(8,128)(2,1)S(1)}, u32[]{:S(2)}, u32[]{:S(2)}) collective-permute-start(bf16[4,32,512]{2,1,0:T(8,128)(2,1)S(1)} %add_convert_fusion.3), channel_id=1, source_target_pairs={{32,0},{64,32},{96,64},{128,96},{160,128},{192,160},{224,192},{33,... | collective-permute-start | bytes 393224 | tf_op jit(solution)/shard_map/ppermute | solution.py:18
  159.4 7.7 %collective-permute-start.4 = (bf16[4,32,512]{2,1,0:T(8,128)(2,1)S(1)}, bf16[4,32,512]{2,1,0:T(8,128)(2,1)S(1)}, u32[]{:S(2)}, u32[]{:S(2)}) collective-permute-start(bf16[4,32,512]{2,1,0:T(8,128)(2,1)S(1)} %add_convert_fusion.2), channel_id=1, source_target_pairs={{32,0},{64,32},{96,64},{128,96},{160,128},{192,160},{224,192},{33,... | collective-permute-start | bytes 393224 | tf_op jit(solution)/shard_map/ppermute | solution.py:18
  167.4 7.6 %collective-permute-start.5 = (bf16[4,32,512]{2,1,0:T(8,128)(2,1)S(1)}, bf16[4,32,512]{2,1,0:T(8,128)(2,1)S(1)}, u32[]{:S(2)}, u32[]{:S(2)}) collective-permute-start(bf16[4,32,512]{2,1,0:T(8,128)(2,1)S(1)} %add_convert_fusion.1), channel_id=1, source_target_pairs={{32,0},{64,32},{96,64},{128,96},{160,128},{192,160},{224,192},{33,... | collective-permute-start | bytes 393224 | tf_op jit(solution)/shard_map/ppermute | solution.py:18
  175.3 7.0 %collective-permute-start.6 = (bf16[4,32,512]{2,1,0:T(8,128)(2,1)S(1)}, bf16[4,32,512]{2,1,0:T(8,128)(2,1)S(1)}, u32[]{:S(2)}, u32[]{:S(2)}) collective-permute-start(bf16[4,32,512]{2,1,0:T(8,128)(2,1)S(1)} %add_convert_fusion), channel_id=1, source_target_pairs={{32,0},{64,32},{96,64},{128,96},{160,128},{192,160},{224,192},{33,... | collective-permute-start | bytes 393224 | tf_op jit(solution)/shard_map/ppermute | solution.py:18
  182.6 3.2 copy-start.4
Sparse Core Ops, SparseCore 0:
  9.9 55.2 all-gather.1
where the time goes:
time: 433 us; the launch traced here: 425 us
  blocking collectives  137 us (32%)
  other arithmetic  93 us (21%)
  matrix products  62.2 us (14%)
  local copies, waits for them, and re-layouts  60.6 us (14%)
  waiting for transfers between devices  38.8 us (9%)
  starting transfers between devices  18.6 us (4%)
  between operations  14.4 us (3%)
    unnamed x1, blocking collectives  120 us
    unnamed x1, other arithmetic  90.6 us
    unnamed x23, local copies, waits for them, and re-layouts  51.5 us
    ppermute x7, waiting for transfers between devices, passed_along(): lax.ppermute(value, axis, [(source, source + steps) for source in range(f...  32.1 us
    dot_general x8, matrix products, one_batch(): jnp.einsum('bde,qde->bq', outer_prod, precond, preferred_element_type=jnp...  30.5 us
    dot_general x8, matrix products, one_batch(): jnp.einsum('btd,bte->bde', grad_block, act_block, preferred_element_type=...  20 us
    psum x1, blocking collectives, body(): mine = lax.psum(mine, 'seg')  16.8 us
    all_to_all x1, starting transfers between devices, body(): lax.all_to_all(train_grads, 'blk', split_axis=2, concat_axis=1, tiled=True)  9.35 us
  transfers between devices with their start and end apart: 9, of which 7 were waited for; matrix products, arithmetic and copies ran while one was open for 38% of the time, Pallas kernels for 0%

commit v1 on v0

v1 whole, which is shorter than its diff:
```python
import jax
import jax.numpy as jnp
from jax import lax
from jax.experimental import pallas as pl
from jax.experimental.pallas import tpu as pltpu
from jax.sharding import PartitionSpec as P

TB = 64
SLOTS = 2
HALF = TB // 2
ROWS = TB + HALF

damping = 0.05
f32 = jnp.float32
bf16 = jnp.bfloat16


def moved_one(value, axis, source, target):
    return lax.ppermute(value, axis, [(source, target)])


def swapped(value, axis):
    return lax.ppermute(value, axis, [(i, i ^ 1) for i in range(lax.axis_size(axis))])


def advance(current, weight, derivs):
    mixed = jnp.dot(current, weight, preferred_element_type=f32)
    return (current.astype(f32) + mixed * derivs.astype(f32)).astype(bf16)


def pack_kernel(count_ref, rows_ref, other_ref, derivs_ref, out_ref, passed_ref):
    width = out_ref.shape[2]
    both = count_ref[0] == SLOTS
    for i in range(out_ref.shape[0]):
        cols = pl.ds(i * width, width)
        out_ref[i, :TB, :] = rows_ref[:TB, cols]
        out_ref[i, TB:, :] = jnp.where(both, rows_ref[TB:ROWS, cols], other_ref[:, cols])
    passed_ref[...] = derivs_ref[...]


def pack(own_count, rows, other, derivs, width, step_slices):
    total = rows.shape[1]
    slices = total // width
    block = step_slices * width
    same = pl.BlockSpec(derivs.shape, lambda i, c: (0, 0))
    return pl.pallas_call(
        pack_kernel,
        grid_spec=pltpu.PrefetchScalarGridSpec(
            num_scalar_prefetch=1,
            grid=(slices // step_slices,),
            in_specs=[
                pl.BlockSpec((ROWS, block), lambda i, c: (0, i)),
                pl.BlockSpec((HALF, block), lambda i, c: (0, i)),
                same,
            ],
            out_specs=[
                pl.BlockSpec((step_slices, ROWS, width), lambda i, c: (i, 0, 0)),
                same,
            ],
        ),
        out_shape=[
            jax.ShapeDtypeStruct((slices, ROWS, width), bf16),
            jax.ShapeDtypeStruct(derivs.shape, bf16),
        ],
        compiler_params=pltpu.CompilerParams(vmem_limit_bytes=32 * 1024 * 1024),
        cost_estimate=pl.CostEstimate(
            flops=0, bytes_accessed=4 * slices * ROWS * width, transcendentals=0
        ),
    )(own_count, rows, other, derivs)


def acts_kernel(count_ref, rows_ref, other_ref, basis_ref, out_ref):
    both = count_ref[0] == SLOTS
    basis = basis_ref[...]
    out_ref[:TB, :] = jnp.dot(rows_ref[:TB, :], basis, preferred_element_type=f32).astype(bf16)
    rest = jnp.where(both, rows_ref[TB:ROWS, :], other_ref[...])
    out_ref[TB:, :] = jnp.dot(rest, basis, preferred_element_type=f32).astype(bf16)


def rotated_acts(own_count, rows, other, basis):
    width = rows.shape[1]
    vmem = pl.BlockSpec(memory_space=pltpu.VMEM)
    return pl.pallas_call(
        acts_kernel,
        in_specs=[pl.BlockSpec(memory_space=pltpu.SMEM), vmem, vmem, vmem],
        out_specs=vmem,
        out_shape=jax.ShapeDtypeStruct((ROWS, width), bf16),
        cost_estimate=pl.CostEstimate(
            flops=2 * ROWS * width * width, bytes_accessed=2 * width * (width + 3 * ROWS), transcendentals=0
        ),
    )(own_count, rows, other, basis)


def core_kernel(err_ref, qacts_ref, bin_ref, bout_ref, eig_ref, core_ref):
    queries = core_ref.shape[0]
    query_tok = err_ref.shape[0] // queries
    rot_err = jnp.dot(err_ref[...], bout_ref[...], preferred_element_type=f32).astype(bf16)
    rot_acts = jnp.dot(qacts_ref[...], bin_ref[...], preferred_element_type=f32).astype(bf16)
    inverse = 1.0 / (eig_ref[...].astype(f32) + damping)
    for q in range(queries):
        tokens = slice(q * query_tok, (q + 1) * query_tok)
        raw = lax.dot_general(
            rot_err[tokens], rot_acts[tokens], (((0,), (0,)), ((), ())),
            preferred_element_type=f32,
        )
        core_ref[q] = (raw * inverse).astype(bf16)


def scaled_core(err, qacts, basis_in, basis_out, eigen, queries):
    width = basis_out.shape[0]
    vmem = pl.BlockSpec(memory_space=pltpu.VMEM)
    return pl.pallas_call(
        core_kernel,
        in_specs=[vmem] * 5,
        out_specs=vmem,
        out_shape=jax.ShapeDtypeStruct((queries, width, width), bf16),
        compiler_params=pltpu.CompilerParams(vmem_limit_bytes=24 * 1024 * 1024),
        cost_estimate=pl.CostEstimate(
            flops=6 * err.shape[0] * width * width,
            bytes_accessed=(6 + 2 * queries) * width * width,
            transcendentals=0,
        ),
    )(err, qacts, basis_in, basis_out, eigen)


def score_kernel(core_ref, bout_ref, place_ref, grads_ref, acts_ref, out_ref, acc_ref):
    step = pl.program_id(0)
    queries = out_ref.shape[0]
    width = bout_ref.shape[0]
    groups = grads_ref.shape[0] // HALF

    grads = jnp.dot(grads_ref[...], bout_ref[...], preferred_element_type=f32).astype(bf16)
    acts = acts_ref[...].astype(f32)
    at = pl.multiple_of(step * groups, groups)
    for q in range(queries):
        mapped = jnp.dot(grads, core_ref[q], preferred_element_type=f32)
        summed = (mapped * acts).reshape(groups, HALF, width).sum(axis=1)
        acc_ref[q, pl.ds(at, groups), :] = summed

    @pl.when(step == pl.num_programs(0) - 1)
    def _():
        for q in range(queries):
            by_slot = jnp.dot(
                place_ref[...], acc_ref[q], precision=lax.Precision.HIGHEST,
                preferred_element_type=f32,
            )
            out_ref[q] = jnp.broadcast_to(
                by_slot.sum(axis=1, keepdims=True), out_ref.shape[1:]
            )


def block_scores(core, basis_out, placement, grads, acts, tile):
    rows, width = grads.shape
    queries = core.shape[0]
    slots = placement.shape[0]
    lanes = 128
    whole = lambda a: pl.BlockSpec(a.shape, lambda i: (0,) * a.ndim)
    streamed = pl.BlockSpec((tile, width), lambda i: (i, 0))
    return pl.pallas_call(
        score_kernel,
        grid=(rows // tile,),
        in_specs=[whole(core), whole(basis_out), whole(placement), streamed, streamed],
        out_specs=pl.BlockSpec((queries, slots, lanes), lambda i: (0, 0, 0)),
        out_shape=jax.ShapeDtypeStruct((queries, slots, lanes), f32),
        scratch_shapes=[pltpu.VMEM((queries, rows // HALF, width), f32)],
        compiler_params=pltpu.CompilerParams(vmem_limit_bytes=48 * 1024 * 1024),
        cost_estimate=pl.CostEstimate(
            flops=2 * rows * width * width * (queries + 1),
            bytes_accessed=4 * rows * width,
            transcendentals=0,
        ),
    )(core, basis_out, placement, grads, acts)


def body(
    train_acts, train_grads, counts, basis_in, basis_out, eigenvalues, back_weight,
    derivative, query_acts, query_top,
):
    seg_count = lax.axis_size("seg")
    seg_index = lax.axis_index("seg")
    blk_count = lax.axis_size("blk")
    blk_index = lax.axis_index("blk")
    queries, query_tok, width = query_top.shape
    own_count = lax.dynamic_slice_in_dim(counts, blk_index, 1)

    pieces = ROWS // HALF
    holder = jnp.arange(blk_count * pieces, dtype=jnp.int32) // pieces
    piece = jnp.arange(blk_count * pieces, dtype=jnp.int32) % pieces
    pair_first = jnp.repeat(counts.reshape(-1, 2)[:, 0] == SLOTS, 2 * pieces)
    extra = (holder // 2) * 2 * SLOTS + jnp.where(pair_first, 1, SLOTS + 1)
    slot_of = jnp.where(piece < TB // HALF, holder * SLOTS, extra)
    slot_ids = jnp.arange(blk_count * SLOTS, dtype=jnp.int32)
    placement = (slot_ids[:, None] == slot_of[None, :]).astype(f32)

    acts_other = swapped(train_acts[0, ROWS:], "blk")
    grads_other = swapped(train_grads[0, ROWS:], "blk")
    acts_own = rotated_acts(own_count, train_acts[0], acts_other, basis_in[0, 0])
    acts_rows = lax.all_gather(acts_own, "blk", axis=0, tiled=True)

    derivs = derivative[0].reshape(queries * query_tok, width)
    packed, late_derivs = pack(own_count, train_grads[0], grads_other, derivs, width, 4)
    grad_rows = lax.all_to_all(packed, "blk", split_axis=0, concat_axis=0, tiled=True)
    grad_rows = grad_rows.reshape(blk_count * ROWS, width)

    current = query_top.reshape(queries * query_tok, width)
    kept = current
    for relay_step in range(seg_count - 1):
        segment = seg_count - 1 - relay_step
        moved = advance(current, back_weight[0, 0], late_derivs if relay_step else derivs)
        current = moved_one(moved, "seg", segment, segment - 1)
        kept = jnp.where(seg_index == segment - 1, current, kept)

    core = scaled_core(
        kept, query_acts[0].reshape(queries * query_tok, width),
        basis_in[0, 0], basis_out[0, 0], eigenvalues[0, 0], queries,
    )
    part = block_scores(core, basis_out[0, 0], placement, grad_rows, acts_rows, 8 * ROWS)
    part = part[:, :, 0].T.reshape(blk_count, SLOTS * queries)
    mine = lax.all_to_all(part, "blk", split_axis=0, concat_axis=0, tiled=True).sum(axis=0)
    copies = jnp.broadcast_to(mine[None], (seg_count, SLOTS * queries))
    mine = lax.all_to_all(copies, "seg", split_axis=0, concat_axis=0, tiled=True).sum(axis=0)
    return mine.reshape(SLOTS, queries).T


def solution(mesh):
    in_specs = (
        P("seg", "blk", None),
        P("seg", "blk", None),
        P(),
        P("seg", None, None, None),
        P("seg", "blk", None, None),
        P("seg", "blk", None, None),
        P("seg", "blk", None, None),
        P("seg", None, None, "blk"),
        P("seg", None, None, None),
        P(None, None, "blk"),
    )
    out_specs = P(None, "blk")
    return jax.shard_map(body, mesh=mesh, in_specs=in_specs, out_specs=out_specs, check_vma=False)
```

time: 433 us -> 128 us (0.30); the launches traced: 425 us -> 128 us
  blocking collectives: 137 us -> 25.4 us
  other arithmetic: 93 us -> 0.27 us
  matrix products: 62.2 us -> 1.67 us
  local copies, waits for them, and re-layouts: 60.6 us -> 12.3 us
  Pallas kernels: 0 us -> 16 us
  waiting for transfers between devices: 38.8 us -> 43.9 us
    unnamed x1 -> x0, blocking collectives: 120 us -> none
    unnamed x1 -> x0, other arithmetic: 90.6 us -> none
    dot_general x28 -> x7, matrix products: 62.2 us -> 1.67 us  [advance(): mixed = jnp.dot(current, weight, preferred_element_type=f32)]
    unnamed x23 -> x24, local copies, waits for them, and re-layouts: 51.5 us -> 7.78 us
    all_to_all x0 -> x2, blocking collectives: none -> 25.4 us  [the longest x1 13.9 us: body(): lax.all_to_all(copies, 'seg', split_axis=0, concat_axis=0, tiled=True)]
    psum x1 -> x0, blocking collectives: 16.8 us -> none  [body(): mine = lax.psum(mine, 'seg')]
    pallas_call x0 -> x4, Pallas kernels: none -> 16 us  [the longest x1 10.9 us: block_scores(): pl.pallas_call(score_kernel, grid=(rows // tile,), in_specs=[whole(core),...]
    all_gather x1, waiting for transfers between devices: 0.01 us -> 6.65 us  [body(): acts_rows = lax.all_gather(acts_own, 'blk', axis=0, tiled=True)]
  transfers between devices with their start and end apart: 9 -> 11, of which waited for: 7 -> 3; matrix products, arithmetic and copies ran while one was open for 38% -> 4% of each run, Pallas kernels for 0% -> 2%
where the time goes in v1:
time: 128 us
  waiting for transfers between devices  43.9 us (34%)
  blocking collectives  25.4 us (20%)
  Pallas kernels  16 us (12%)
  starting transfers between devices  14.4 us (11%)
  between operations  13.7 us (11%)
  local copies, waits for them, and re-layouts  12.3 us (10%)
  matrix products  1.67 us (1%)
    ppermute x7, waiting for transfers between devices, moved_one(): return lax.ppermute(value, axis, [(source, target)])  34.6 us
    all_to_all x1, blocking collectives, body(): lax.all_to_all(copies, 'seg', split_axis=0, concat_axis=0, tiled=True)  13.9 us
    all_to_all x1, blocking collectives, body(): lax.all_to_all(part, 'blk', split_axis=0, concat_axis=0, tiled=True)  11.6 us
    pallas_call x1, Pallas kernels, block_scores(): pl.pallas_call(score_kernel, grid=(rows // tile,), in_specs=[whole(core),...  10.9 us
    unnamed x24, local copies, waits for them, and re-layouts  7.78 us
    all_gather x1, waiting for transfers between devices, body(): acts_rows = lax.all_gather(acts_own, 'blk', axis=0, tiled=True)  6.65 us
    all_to_all x1, starting transfers between devices, body(): lax.all_to_all(packed, 'blk', split_axis=0, concat_axis=0, tiled=True)  5.68 us
    ppermute x7, starting transfers between devices, moved_one(): return lax.ppermute(value, axis, [(source, target)])  5.44 us
  transfers between devices with their start and end apart: 11, of which 3 were waited for; matrix products, arithmetic and copies ran while one was open for 4% of the time, Pallas kernels for 2%

profile of v1, /device:TPU:1, one launch (start us, length us, event | category | flops | bytes accessed | tf_op | source)
XLA Modules:
  0.0 127.7 jit_solution(13776093357898597635)
XLA Ops:
  6.5 0.8 slice_bitcast_fusion.1
  7.4 3.2 %collective-permute-start.8 = (bf16[32,512]{1,0:T(8,128)(2,1)S(1)}, bf16[32,512]{1,0:T(8,128)(2,1)S(1)}, u32[]{:S(2)}, u32[]{:S(2)}) collective-permute-start(bf16[32,512]{1,0:T(8,128)(2,1)S(1)} %slice_bitcast_fusion.1), channel_id=1, source_target_pairs={{0,1},{1,0},{2,3},{3,2},{4,5},{5,4},{6,7},{7,6},{8,9},{9,8},{10,11... | collective-permute-start | bytes 98312 | tf_op jit(solution)/shard_map/ppermute | solution.py:23
  10.6 1.2 dynamic_slice.3.count_ref
  11.9 0.6 copy-done.10
  12.4 2.7 %shard_map.102 = bf16[96,512]{1,0:T(8,128)(2,1)} custom-call(s32[1]{0:T(128)} %dynamic_slice.3.count_ref, bf16[128,512]{1,0:T(8,128)(2,1)} %bitcast.62, bf16[32,512]{1,0:T(8,128)(2,1)} %copy-done.10, bf16[512,512]{1,0:T(8,128)(2,1)} %bitcast.53), custom_call_target="tpu_custom_call" | custom-call | flops 50331648 | bytes 819200 | tf_op jit(solution)/shard_map/pallas_call | solution.py:83
  15.2 1.3 %slice_bitcast_fusion = bf16[32,16384]{1,0:T(8,128)(2,1)S(1)} fusion(bf16[1,128,16384]{2,1,0:T(8,128)(2,1)} %param.11), kind=kLoop, calls=%fused_computation.9 | loop fusion | bytes 2097152 | tf_op jit(solution)/shard_map/squeeze | solution.py:196
  16.6 2.6 %collective-permute-done.1.other_ref = bf16[32,16384]{1,0:T(8,128)(2,1)S(1)} collective-permute-done((bf16[32,16384]{1,0:T(8,128)(2,1)S(1)}, bf16[32,16384]{1,0:T(8,128)(2,1)S(1)}, u32[]{:S(2)}, u32[]{:S(2)}) %collective-permute-start.1) | collective-permute-done | bytes 1048608 | tf_op jit(solution)/shard_map/ppermute | solution.py:23
  19.2 2.2 %copy-done.1 = bf16[1,128,16384]{2,1,0:T(8,128)(2,1)S(1)} copy-done((bf16[1,128,16384]{2,1,0:T(8,128)(2,1)S(1)}, bf16[1,128,16384]{2,1,0:T(8,128)(2,1)}, u32[]{:S(2)}) %copy-start.1) | copy-done | bytes 4194328
  21.4 1.4 %shard_map.100 = (bf16[32,96,512]{2,1,0:T(8,128)(2,1)S(1)}, bf16[128,512]{1,0:T(8,128)(2,1)S(1)}) custom-call(s32[1]{0:T(128)} %dynamic_slice.3.count_ref, bf16[128,16384]{1,0:T(8,128)(2,1)S(1)} %bitcast.52, bf16[32,16384]{1,0:T(8,128)(2,1)S(1)} %collective-permute-done.1.other_ref, bf16[128,512]{1,0:T(8,128)(2,1)S(1)} %bitcast.58), custom_call_target="tpu_custom_call" | custom-call | bytes 6291456 | tf_op jit(solution)/shard_map/pallas_call | solution.py:46
  22.8 1.7 %copy-done.2 = bf16[32,96,512]{2,1,0:T(8,128)(2,1)} copy-done((bf16[32,96,512]{2,1,0:T(8,128)(2,1)}, bf16[32,96,512]{2,1,0:T(8,128)(2,1)S(1)}, u32[]{:S(2)}) %copy-start.2) | copy-done | bytes 3145752
  24.5 5.7 %all-to-all-start = ((bf16[32,96,512]{2,1,0:T(8,128)(2,1)}), bf16[32,96,512]{2,1,0:T(8,128)(2,1)}, u32[]{:S(2)}, u32[]{:S(2)}) async-start(bf16[32,96,512]{2,1,0:T(8,128)(2,1)} %copy-done.2), calls=%async_computation | async-start | bytes 6291456 | tf_op jit(solution)/shard_map/all_to_all | solution.py:202
  30.5 0.7 collective-permute-start
  31.2 0.2 add_convert_fusion.5
  31.4 0.8 collective-permute-start.2
  32.3 0.2 add_convert_fusion.4
  32.5 0.7 collective-permute-start.3
  33.2 0.2 add_convert_fusion.3
  33.4 0.7 collective-permute-start.4
  34.1 0.2 add_convert_fusion.2
  34.4 0.7 collective-permute-start.5
  35.7 0.7 collective-permute-start.6
  36.7 1.3 %collective-permute-start.7 = (bf16[128,512]{1,0:T(8,128)(2,1)S(1)}, bf16[128,512]{1,0:T(8,128)(2,1)S(1)}, u32[]{:S(2)}, u32[]{:S(2)}) collective-permute-start(bf16[128,512]{1,0:T(8,128)(2,1)S(1)} %add_convert_fusion), channel_id=1, source_target_pairs={{32,0},{33,1},{34,2},{35,3},{36,4},{37,5},{38,6},{39,7},{40,8},{41... | collective-permute-start | bytes 393224 | tf_op jit(solution)/shard_map/ppermute | solution.py:19
  38.0 34.5 %collective-permute-done.7 = bf16[128,512]{1,0:T(8,128)(2,1)S(1)} collective-permute-done((bf16[128,512]{1,0:T(8,128)(2,1)S(1)}, bf16[128,512]{1,0:T(8,128)(2,1)S(1)}, u32[]{:S(2)}, u32[]{:S(2)}) %collective-permute-start.7) | collective-permute-done | bytes 131104 | tf_op jit(solution)/shard_map/ppermute | solution.py:19
  72.6 1.1 copy-done.4
  73.7 1.1 copy-done.5
  74.8 1.0 shard_map.101.core_ref
  75.8 6.7 %all-gather.2.cloned.1.call-done.acts_ref = bf16[3072,512]{1,0:T(8,128)(2,1)} async-done(((bf16[96,512]{1,0:T(8,128)(2,1)}), bf16[3072,512]{1,0:T(8,128)(2,1)}) %all-gather.2.cloned.1.call-update) | async-done | bytes 3145744 | tf_op jit(solution)/shard_map/all_gather | solution.py:198
  82.5 1.0 copy-done.6
  83.5 10.9 %shard_map.103 = f32[4,64,128]{2,1,0:T(8,128)S(1)} custom-call(bf16[4,512,512]{2,1,0:T(8,128)(2,1)S(1)} %shard_map.101.core_ref, bf16[512,512]{1,0:T(8,128)(2,1)S(1)} %bitcast.57, f32[64,96]{1,0:T(8,128)S(1)} %fusion.9.place_ref, bf16[3072,512]{1,0:T(8,128)(2,1)} %bitcast.9.grads_ref, bf16[3072,512]{1,0:T(8,128)(2,1)} %all-gather.2.cloned.1.call-done.acts_ref), custom_call_target="tpu_custom_call" | custom-call | flops 8053063680 | bytes 6291456 | tf_op jit(solution)/shard_map/pallas_call | solution.py:159
  94.7 11.6 %all_to_all.20 = f32[32,1,8]{2,1,0:T(1,128)S(1)} all-to-all(f32[32,1,8]{2,1,0:T(1,128)S(1)} %bitcast.63), channel_id=1, replica_groups=mesh['seg'=8,'blk'=32] {'blk'}, dimensions={0} | all-to-all | bytes 2048 | tf_op jit(solution)/shard_map/all_to_all | solution.py:219
  106.3 13.9 %all_to_all.21 = f32[8,1,8]{2,1,0:T(1,128)S(1)} all-to-all(f32[8,1,8]{2,1,0:T(1,128)S(1)} %broadcast_in_dim.9), channel_id=1, replica_groups=mesh['seg'=8,'blk'=32] {'seg'}, dimensions={0} | all-to-all | bytes 512 | tf_op jit(solution)/shard_map/all_to_all | solution.py:221
  120.2 0.6 reshape.78
  (45 shorter events, 1.7 us)
Async XLA Ops:
  6.5 23.7 %copy-start = (bf16[1,1,512,512]{3,2,1,0:T(8,128)(2,1)S(1)}, bf16[1,1,512,512]{3,2,1,0:T(8,128)(2,1)}, u32[]{:S(2)}) copy-start(bf16[1,1,512,512]{3,2,1,0:T(8,128)(2,1)} %param.16) | copy-start | bytes 1572868
  6.5 12.7 %copy-start.7 = (bf16[1,4,32,512]{3,2,1,0:T(8,128)(2,1)S(1)}, bf16[1,4,32,512]{3,2,1,0:T(8,128)(2,1)}, u32[]{:S(2)}) copy-start(bf16[1,4,32,512]{3,2,1,0:T(8,128)(2,1)} %param.17) | copy-start | bytes 393220
  6.5 75.9 %all-gather.2.cloned.1.call-start = ((), (), s32[]{:S(2)}) async-start(), calls=%async_computation.3 | async-start | bytes 3244032 | tf_op jit(solution)/shard_map/all_gather | solution.py:198
  7.4 4.5 %collective-permute-start.8 = (bf16[32,512]{1,0:T(8,128)(2,1)S(1)}, bf16[32,512]{1,0:T(8,128)(2,1)S(1)}, u32[]{:S(2)}, u32[]{:S(2)}) collective-permute-start(bf16[32,512]{1,0:T(8,128)(2,1)S(1)} %slice_bitcast_fusion.1), channel_id=1, source_target_pairs={{0,1},{1,0},{2,3},{3,2},{4,5},{5,4},{6,7},{7,6},{8,9},{9,8},{10,11... | collective-permute-start | bytes 98312 | tf_op jit(solution)/shard_map/ppermute | solution.py:23
  11.8 0.6 copy-start.10
  16.5 2.7 %collective-permute-start.1 = (bf16[32,16384]{1,0:T(8,128)(2,1)S(1)}, bf16[32,16384]{1,0:T(8,128)(2,1)S(1)}, u32[]{:S(2)}, u32[]{:S(2)}) collective-permute-start(bf16[32,16384]{1,0:T(8,128)(2,1)S(1)} %slice_bitcast_fusion), channel_id=1, source_target_pairs={{0,1},{1,0},{2,3},{3,2},{4,5},{5,4},{6,7},{7,6},{8,9},{9,8},{10,11... | collective-permute-start | bytes 3145736 | tf_op jit(solution)/shard_map/ppermute | solution.py:23
  19.2 2.2 %copy-start.1 = (bf16[1,128,16384]{2,1,0:T(8,128)(2,1)S(1)}, bf16[1,128,16384]{2,1,0:T(8,128)(2,1)}, u32[]{:S(2)}) copy-start(bf16[1,128,16384]{2,1,0:T(8,128)(2,1)} %param.11) | copy-start | bytes 12582916
  22.8 1.7 %copy-start.2 = (bf16[32,96,512]{2,1,0:T(8,128)(2,1)}, bf16[32,96,512]{2,1,0:T(8,128)(2,1)S(1)}, u32[]{:S(2)}) copy-start(bf16[32,96,512]{2,1,0:T(8,128)(2,1)S(1)} %get-tuple-element.8) | copy-start | bytes 9437188
  24.5 5.7 %copy-start.9 = (bf16[4,32,512]{2,1,0:T(8,128)(2,1)S(1)}, bf16[4,32,512]{2,1,0:T(8,128)(2,1)}, u32[]{:S(2)}) copy-start(bf16[4,32,512]{2,1,0:T(8,128)(2,1)} %param.19) | copy-start | bytes 393220
  24.5 51.3 %all-to-all-start = ((bf16[32,96,512]{2,1,0:T(8,128)(2,1)}), bf16[32,96,512]{2,1,0:T(8,128)(2,1)}, u32[]{:S(2)}, u32[]{:S(2)}) async-start(bf16[32,96,512]{2,1,0:T(8,128)(2,1)} %copy-done.2), calls=%async_computation | async-start | bytes 6291456 | tf_op jit(solution)/shard_map/all_to_all | solution.py:202
  30.2 4.8 %copy-start.11 = (s32[32]{0:T(128)S(1)}, s32[32]{0:T(128)}, u32[]{:S(2)}) copy-start(s32[32]{0:T(128)} %param.12) | copy-start | bytes 388
  30.5 0.7 collective-permute-start
  31.4 41.2 %copy-start.3 = (bf16[1,1,512,512]{3,2,1,0:T(8,128)(2,1)S(1)}, bf16[1,1,512,512]{3,2,1,0:T(8,128)(2,1)}, u32[]{:S(2)}) copy-start(bf16[1,1,512,512]{3,2,1,0:T(8,128)(2,1)} %param.13) | copy-start | bytes 1572868
  31.4 41.2 %copy-start.8 = (bf16[1,4,32,512]{3,2,1,0:T(8,128)(2,1)S(1)}, bf16[1,4,32,512]{3,2,1,0:T(8,128)(2,1)}, u32[]{:S(2)}) copy-start(bf16[1,4,32,512]{3,2,1,0:T(8,128)(2,1)} %param.18) | copy-start | bytes 393220
  31.4 0.8 collective-permute-start.2
  32.5 0.7 collective-permute-start.3
  33.4 0.7 collective-permute-start.4
  34.4 1.1 collective-permute-start.5
  35.7 0.7 collective-permute-start.6
  36.7 35.9 %collective-permute-start.7 = (bf16[128,512]{1,0:T(8,128)(2,1)S(1)}, bf16[128,512]{1,0:T(8,128)(2,1)S(1)}, u32[]{:S(2)}, u32[]{:S(2)}) collective-permute-start(bf16[128,512]{1,0:T(8,128)(2,1)S(1)} %add_convert_fusion), channel_id=1, source_target_pairs={{32,0},{33,1},{34,2},{35,3},{36,4},{37,5},{38,6},{39,7},{40,8},{41... | collective-permute-start | bytes 393224 | tf_op jit(solution)/shard_map/ppermute | solution.py:19
  72.6 1.1 copy-start.4
  73.7 1.1 copy-start.5
  82.4 1.0 copy-start.6
Sparse Core Ops, SparseCore 0:
  15.3 67.0 all-gather.1

commit v2 on v1

--- a/solution.py
+++ b/solution.py
@@ -30,7 +30,7 @@
 
 def pack_kernel(count_ref, rows_ref, other_ref, derivs_ref, out_ref, passed_ref):
     width = out_ref.shape[2]
-    both = count_ref[0] == SLOTS
+    both = count_ref[lax.axis_index("blk")] == SLOTS
     for i in range(out_ref.shape[0]):
         cols = pl.ds(i * width, width)
         out_ref[i, :TB, :] = rows_ref[:TB, cols]
@@ -38,7 +38,7 @@
     passed_ref[...] = derivs_ref[...]
 
 
-def pack(own_count, rows, other, derivs, width, step_slices):
+def pack(all_counts, rows, other, derivs, width, step_slices):
     total = rows.shape[1]
     slices = total // width
     block = step_slices * width
@@ -66,18 +66,18 @@
         cost_estimate=pl.CostEstimate(
             flops=0, bytes_accessed=4 * slices * ROWS * width, transcendentals=0
         ),
-    )(own_count, rows, other, derivs)
+    )(all_counts, rows, other, derivs)
 
 
 def acts_kernel(count_ref, rows_ref, other_ref, basis_ref, out_ref):
-    both = count_ref[0] == SLOTS
+    both = count_ref[lax.axis_index("blk")] == SLOTS
     basis = basis_ref[...]
     out_ref[:TB, :] = jnp.dot(rows_ref[:TB, :], basis, preferred_element_type=f32).astype(bf16)
     rest = jnp.where(both, rows_ref[TB:ROWS, :], other_ref[...])
     out_ref[TB:, :] = jnp.dot(rest, basis, preferred_element_type=f32).astype(bf16)
 
 
-def rotated_acts(own_count, rows, other, basis):
+def rotated_acts(all_counts, rows, other, basis):
     width = rows.shape[1]
     vmem = pl.BlockSpec(memory_space=pltpu.VMEM)
     return pl.pallas_call(
@@ -88,7 +88,7 @@
         cost_estimate=pl.CostEstimate(
             flops=2 * ROWS * width * width, bytes_accessed=2 * width * (width + 3 * ROWS), transcendentals=0
         ),
-    )(own_count, rows, other, basis)
+    )(all_counts, rows, other, basis)
 
 
 def core_kernel(err_ref, qacts_ref, bin_ref, bout_ref, eig_ref, core_ref):
@@ -181,7 +181,7 @@
     blk_count = lax.axis_size("blk")
     blk_index = lax.axis_index("blk")
     queries, query_tok, width = query_top.shape
-    own_count = lax.dynamic_slice_in_dim(counts, blk_index, 1)
+    all_counts = counts
 
     pieces = ROWS // HALF
     holder = jnp.arange(blk_count * pieces, dtype=jnp.int32) // pieces
@@ -194,11 +194,11 @@
 
     acts_other = swapped(train_acts[0, ROWS:], "blk")
     grads_other = swapped(train_grads[0, ROWS:], "blk")
-    acts_own = rotated_acts(own_count, train_acts[0], acts_other, basis_in[0, 0])
+    acts_own = rotated_acts(all_counts, train_acts[0], acts_other, basis_in[0, 0])
     acts_rows = lax.all_gather(acts_own, "blk", axis=0, tiled=True)
 
     derivs = derivative[0].reshape(queries * query_tok, width)
-    packed, late_derivs = pack(own_count, train_grads[0], grads_other, derivs, width, 4)
+    packed, late_derivs = pack(all_counts, train_grads[0], grads_other, derivs, width, 4)
     grad_rows = lax.all_to_all(packed, "blk", split_axis=0, concat_axis=0, tiled=True)
     grad_rows = grad_rows.reshape(blk_count * ROWS, width)
 

time: 128 us -> 128 us (level)
    unnamed x24 -> x26, local copies, waits for them, and re-layouts: 7.78 us -> 8.39 us
  transfers between devices with their start and end apart: 11 -> 11, of which waited for: 3 -> 4; matrix products, arithmetic and copies ran while one was open for 4% -> 3% of each run, Pallas kernels for 2% -> 2%
where the time goes in v2:
time: 128 us; the launch traced here: 127 us
  waiting for transfers between devices  44.4 us (35%)
  blocking collectives  25.3 us (20%)
  Pallas kernels  15.2 us (12%)
  starting transfers between devices  15 us (12%)
  between operations  13.7 us (11%)
  local copies, waits for them, and re-layouts  11.7 us (9%)
  matrix products  1.67 us (1%)
    ppermute x7, waiting for transfers between devices, moved_one(): return lax.ppermute(value, axis, [(source, target)])  34.6 us
    all_to_all x1, blocking collectives, body(): lax.all_to_all(copies, 'seg', split_axis=0, concat_axis=0, tiled=True)  14 us
    all_to_all x1, blocking collectives, body(): lax.all_to_all(part, 'blk', split_axis=0, concat_axis=0, tiled=True)  11.3 us
    pallas_call x1, Pallas kernels, block_scores(): pl.pallas_call(score_kernel, grid=(rows // tile,), in_specs=[whole(core),...  10.9 us
    unnamed x26, local copies, waits for them, and re-layouts  8.39 us
    all_gather x1, waiting for transfers between devices, body(): acts_rows = lax.all_gather(acts_own, 'blk', axis=0, tiled=True)  6.6 us
    all_to_all x1, starting transfers between devices, body(): lax.all_to_all(packed, 'blk', split_axis=0, concat_axis=0, tiled=True)  5.87 us
    ppermute x7, starting transfers between devices, moved_one(): return lax.ppermute(value, axis, [(source, target)])  5.44 us
  transfers between devices with their start and end apart: 11, of which 4 were waited for; matrix products, arithmetic and copies ran while one was open for 3% of the time, Pallas kernels for 2%

profile of v2, /device:TPU:1, one launch (start us, length us, event | category | flops | bytes accessed | tf_op | source)
XLA Modules:
  0.0 127.2 jit_solution(10437460707473010203)
XLA Ops:
  6.5 0.8 slice_bitcast_fusion.1
  7.4 3.2 %collective-permute-start.8 = (bf16[32,512]{1,0:T(8,128)(2,1)S(1)}, bf16[32,512]{1,0:T(8,128)(2,1)S(1)}, u32[]{:S(2)}, u32[]{:S(2)}) collective-permute-start(bf16[32,512]{1,0:T(8,128)(2,1)S(1)} %slice_bitcast_fusion.1), channel_id=1, source_target_pairs={{0,1},{1,0},{2,3},{3,2},{4,5},{5,4},{6,7},{7,6},{8,9},{9,8},{10,11... | collective-permute-start | bytes 98312 | tf_op jit(solution)/shard_map/ppermute | solution.py:23
  10.6 0.9 collective-permute-done.8.other_ref
  11.5 0.6 copy-done.12
  12.1 2.1 %shard_map.102 = bf16[96,512]{1,0:T(8,128)(2,1)} custom-call(s32[32]{0:T(128)} %count_ref.3, bf16[128,512]{1,0:T(8,128)(2,1)} %bitcast.62, bf16[32,512]{1,0:T(8,128)(2,1)} %copy-done.12, bf16[512,512]{1,0:T(8,128)(2,1)} %bitcast.53), custom_call_target="tpu_custom_call" | custom-call | flops 50331648 | bytes 819200 | tf_op jit(solution)/shard_map/pallas_call | solution.py:83
  14.2 1.3 %slice_bitcast_fusion = bf16[32,16384]{1,0:T(8,128)(2,1)S(1)} fusion(bf16[1,128,16384]{2,1,0:T(8,128)(2,1)} %param.11), kind=kLoop, calls=%fused_computation.9 | loop fusion | bytes 2097152 | tf_op jit(solution)/shard_map/squeeze | solution.py:196
  15.5 0.4 collective-permute-start.1
  15.9 2.3 %collective-permute-done.1.other_ref = bf16[32,16384]{1,0:T(8,128)(2,1)S(1)} collective-permute-done((bf16[32,16384]{1,0:T(8,128)(2,1)S(1)}, bf16[32,16384]{1,0:T(8,128)(2,1)S(1)}, u32[]{:S(2)}, u32[]{:S(2)}) %collective-permute-start.1) | collective-permute-done | bytes 1048608 | tf_op jit(solution)/shard_map/ppermute | solution.py:23
  18.2 2.2 %copy-done.1 = bf16[1,128,16384]{2,1,0:T(8,128)(2,1)S(1)} copy-done((bf16[1,128,16384]{2,1,0:T(8,128)(2,1)S(1)}, bf16[1,128,16384]{2,1,0:T(8,128)(2,1)}, u32[]{:S(2)}) %copy-start.1) | copy-done | bytes 4194328
  20.4 0.7 copy-done.9
  21.1 1.3 %shard_map.100 = (bf16[32,96,512]{2,1,0:T(8,128)(2,1)S(1)}, bf16[128,512]{1,0:T(8,128)(2,1)S(1)}) custom-call(s32[32]{0:T(128)S(1)} %copy-done.9, bf16[128,16384]{1,0:T(8,128)(2,1)S(1)} %bitcast.52, bf16[32,16384]{1,0:T(8,128)(2,1)S(1)} %collective-permute-done.1.other_ref, bf16[128,512]{1,0:T(8,128)(2,1)S(1)} %bitcast.58), custom_call_target="tpu_custom_call" | custom-call | bytes 6291456 | tf_op jit(solution)/shard_map/pallas_call | solution.py:46
  22.4 1.7 %copy-done.2 = bf16[32,96,512]{2,1,0:T(8,128)(2,1)} copy-done((bf16[32,96,512]{2,1,0:T(8,128)(2,1)}, bf16[32,96,512]{2,1,0:T(8,128)(2,1)S(1)}, u32[]{:S(2)}) %copy-start.2) | copy-done | bytes 3145752
  24.1 5.9 %all-to-all-start = ((bf16[32,96,512]{2,1,0:T(8,128)(2,1)}), bf16[32,96,512]{2,1,0:T(8,128)(2,1)}, u32[]{:S(2)}, u32[]{:S(2)}) async-start(bf16[32,96,512]{2,1,0:T(8,128)(2,1)} %copy-done.2), calls=%async_computation | async-start | bytes 6291456 | tf_op jit(solution)/shard_map/all_to_all | solution.py:202
  30.2 0.7 collective-permute-start
  30.9 0.2 add_convert_fusion.5
  31.2 0.8 collective-permute-start.2
  32.2 0.7 collective-permute-start.3
  33.2 0.7 collective-permute-start.4
  34.1 0.7 collective-permute-start.5
  35.4 0.7 collective-permute-start.6
  36.1 0.2 add_convert_fusion
  36.4 1.3 %collective-permute-start.7 = (bf16[128,512]{1,0:T(8,128)(2,1)S(1)}, bf16[128,512]{1,0:T(8,128)(2,1)S(1)}, u32[]{:S(2)}, u32[]{:S(2)}) collective-permute-start(bf16[128,512]{1,0:T(8,128)(2,1)S(1)} %add_convert_fusion), channel_id=1, source_target_pairs={{32,0},{33,1},{34,2},{35,3},{36,4},{37,5},{38,6},{39,7},{40,8},{41... | collective-permute-start | bytes 393224 | tf_op jit(solution)/shard_map/ppermute | solution.py:19
  37.7 34.5 %collective-permute-done.7 = bf16[128,512]{1,0:T(8,128)(2,1)S(1)} collective-permute-done((bf16[128,512]{1,0:T(8,128)(2,1)S(1)}, bf16[128,512]{1,0:T(8,128)(2,1)S(1)}, u32[]{:S(2)}, u32[]{:S(2)}) %collective-permute-start.7) | collective-permute-done | bytes 131104 | tf_op jit(solution)/shard_map/ppermute | solution.py:19
  72.4 1.1 copy-done.4
  73.4 1.1 copy-done.5
  74.5 1.0 shard_map.101.core_ref
  75.5 6.6 %all-gather.2.cloned.1.call-done.acts_ref = bf16[3072,512]{1,0:T(8,128)(2,1)} async-done(((bf16[96,512]{1,0:T(8,128)(2,1)}), bf16[3072,512]{1,0:T(8,128)(2,1)}) %all-gather.2.cloned.1.call-update) | async-done | bytes 3145744 | tf_op jit(solution)/shard_map/all_gather | solution.py:198
  82.1 1.0 copy-done.6
  83.1 10.9 %shard_map.103 = f32[4,64,128]{2,1,0:T(8,128)S(1)} custom-call(bf16[4,512,512]{2,1,0:T(8,128)(2,1)S(1)} %shard_map.101.core_ref, bf16[512,512]{1,0:T(8,128)(2,1)S(1)} %bitcast.57, f32[64,96]{1,0:T(8,128)S(1)} %fusion.9.place_ref, bf16[3072,512]{1,0:T(8,128)(2,1)} %bitcast.9.grads_ref, bf16[3072,512]{1,0:T(8,128)(2,1)} %all-gather.2.cloned.1.call-done.acts_ref), custom_call_target="tpu_custom_call" | custom-call | flops 8053063680 | bytes 6291456 | tf_op jit(solution)/shard_map/pallas_call | solution.py:159
  94.4 11.3 %all_to_all.20 = f32[32,1,8]{2,1,0:T(1,128)S(1)} all-to-all(f32[32,1,8]{2,1,0:T(1,128)S(1)} %bitcast.63), channel_id=1, replica_groups=mesh['seg'=8,'blk'=32] {'blk'}, dimensions={0} | all-to-all | bytes 2048 | tf_op jit(solution)/shard_map/all_to_all | solution.py:219
  105.7 14.0 %all_to_all.21 = f32[8,1,8]{2,1,0:T(1,128)S(1)} all-to-all(f32[8,1,8]{2,1,0:T(1,128)S(1)} %broadcast_in_dim.9), channel_id=1, replica_groups=mesh['seg'=8,'blk'=32] {'seg'}, dimensions={0} | all-to-all | bytes 512 | tf_op jit(solution)/shard_map/all_to_all | solution.py:221
  119.8 0.6 reshape.78
  (46 shorter events, 2.1 us)
Async XLA Ops:
  6.5 23.4 %copy-start = (bf16[1,1,512,512]{3,2,1,0:T(8,128)(2,1)S(1)}, bf16[1,1,512,512]{3,2,1,0:T(8,128)(2,1)}, u32[]{:S(2)}) copy-start(bf16[1,1,512,512]{3,2,1,0:T(8,128)(2,1)} %param.16) | copy-start | bytes 1572868
  6.5 11.7 %copy-start.7 = (bf16[1,4,32,512]{3,2,1,0:T(8,128)(2,1)S(1)}, bf16[1,4,32,512]{3,2,1,0:T(8,128)(2,1)}, u32[]{:S(2)}) copy-start(bf16[1,4,32,512]{3,2,1,0:T(8,128)(2,1)} %param.17) | copy-start | bytes 393220
  6.5 75.6 %all-gather.2.cloned.1.call-start = ((), (), s32[]{:S(2)}) async-start(), calls=%async_computation.3 | async-start | bytes 3244032 | tf_op jit(solution)/shard_map/all_gather | solution.py:198
  7.4 4.1 %collective-permute-start.8 = (bf16[32,512]{1,0:T(8,128)(2,1)S(1)}, bf16[32,512]{1,0:T(8,128)(2,1)S(1)}, u32[]{:S(2)}, u32[]{:S(2)}) collective-permute-start(bf16[32,512]{1,0:T(8,128)(2,1)S(1)} %slice_bitcast_fusion.1), channel_id=1, source_target_pairs={{0,1},{1,0},{2,3},{3,2},{4,5},{5,4},{6,7},{7,6},{8,9},{9,8},{10,11... | collective-permute-start | bytes 98312 | tf_op jit(solution)/shard_map/ppermute | solution.py:23
  11.5 0.6 copy-start.12
  15.5 2.7 %collective-permute-start.1 = (bf16[32,16384]{1,0:T(8,128)(2,1)S(1)}, bf16[32,16384]{1,0:T(8,128)(2,1)S(1)}, u32[]{:S(2)}, u32[]{:S(2)}) collective-permute-start(bf16[32,16384]{1,0:T(8,128)(2,1)S(1)} %slice_bitcast_fusion), channel_id=1, source_target_pairs={{0,1},{1,0},{2,3},{3,2},{4,5},{5,4},{6,7},{7,6},{8,9},{9,8},{10,11... | collective-permute-start | bytes 3145736 | tf_op jit(solution)/shard_map/ppermute | solution.py:23
  18.2 2.2 %copy-start.1 = (bf16[1,128,16384]{2,1,0:T(8,128)(2,1)S(1)}, bf16[1,128,16384]{2,1,0:T(8,128)(2,1)}, u32[]{:S(2)}) copy-start(bf16[1,128,16384]{2,1,0:T(8,128)(2,1)} %param.11) | copy-start | bytes 12582916
  20.4 0.7 copy-start.9
  22.3 1.7 %copy-start.2 = (bf16[32,96,512]{2,1,0:T(8,128)(2,1)}, bf16[32,96,512]{2,1,0:T(8,128)(2,1)S(1)}, u32[]{:S(2)}) copy-start(bf16[32,96,512]{2,1,0:T(8,128)(2,1)S(1)} %get-tuple-element.8) | copy-start | bytes 9437188
  24.1 5.9 %copy-start.11 = (bf16[4,32,512]{2,1,0:T(8,128)(2,1)S(1)}, bf16[4,32,512]{2,1,0:T(8,128)(2,1)}, u32[]{:S(2)}) copy-start(bf16[4,32,512]{2,1,0:T(8,128)(2,1)} %param.19) | copy-start | bytes 393220
  24.1 51.4 %all-to-all-start = ((bf16[32,96,512]{2,1,0:T(8,128)(2,1)}), bf16[32,96,512]{2,1,0:T(8,128)(2,1)}, u32[]{:S(2)}, u32[]{:S(2)}) async-start(bf16[32,96,512]{2,1,0:T(8,128)(2,1)} %copy-done.2), calls=%async_computation | async-start | bytes 6291456 | tf_op jit(solution)/shard_map/all_to_all | solution.py:202
  29.9 4.9 %copy-start.10 = (s32[32]{0:T(128)S(1)}, s32[32]{0:T(128)}, u32[]{:S(2)}) copy-start(s32[32]{0:T(128)} %count_ref.3) | copy-start | bytes 388
  30.2 0.7 collective-permute-start
  31.1 41.2 %copy-start.3 = (bf16[1,1,512,512]{3,2,1,0:T(8,128)(2,1)S(1)}, bf16[1,1,512,512]{3,2,1,0:T(8,128)(2,1)}, u32[]{:S(2)}) copy-start(bf16[1,1,512,512]{3,2,1,0:T(8,128)(2,1)} %param.13) | copy-start | bytes 1572868
  31.2 41.2 %copy-start.8 = (bf16[1,4,32,512]{3,2,1,0:T(8,128)(2,1)S(1)}, bf16[1,4,32,512]{3,2,1,0:T(8,128)(2,1)}, u32[]{:S(2)}) copy-start(bf16[1,4,32,512]{3,2,1,0:T(8,128)(2,1)} %param.18) | copy-start | bytes 393220
  31.2 0.8 collective-permute-start.2
  32.2 0.7 collective-permute-start.3
  33.2 0.7 collective-permute-start.4
  34.1 1.1 collective-permute-start.5
  35.4 0.7 collective-permute-start.6
  36.4 35.9 %collective-permute-start.7 = (bf16[128,512]{1,0:T(8,128)(2,1)S(1)}, bf16[128,512]{1,0:T(8,128)(2,1)S(1)}, u32[]{:S(2)}, u32[]{:S(2)}) collective-permute-start(bf16[128,512]{1,0:T(8,128)(2,1)S(1)} %add_convert_fusion), channel_id=1, source_target_pairs={{32,0},{33,1},{34,2},{35,3},{36,4},{37,5},{38,6},{39,7},{40,8},{41... | collective-permute-start | bytes 393224 | tf_op jit(solution)/shard_map/ppermute | solution.py:19
  72.3 1.1 copy-start.4
  73.4 1.1 copy-start.5
  82.1 1.0 copy-start.6
Sparse Core Ops, SparseCore 0:
  14.3 67.7 all-gather.1
